TPU v7x, 32 devices: a whole 2x2x4 slice. The times are simulated.
32 devices in a mesh: row: 8 (over y, x, core), col: 4 (over z).
Axes of the slice: x: 2, y: 2, z: 4, core: 2. Of those that a mesh axis runs over, the one named last changes fastest.
Arguments:
- density_matrix: bfloat16 [4096, 4096], P('row', 'col'), may hold values from -1 to 1
- block_mask: int32 [32, 32], P('row', 'col'), may hold values 0 or 1
- cell_group: int32 [256, 256], P('row', 'col'), may hold values from 0 to 31
- electron_shape: float32 [256, 256, 256], P('row', 'col'), may hold values from 0.5 to 20
- ion_charge: float32 [256, 256, 256], P('row', 'col'), may hold values from 0.1 to 6
Outputs:
- next_density: bfloat16 [4096, 4096], P('row', 'col')
- potential: float32 [256, 256, 256], P('row', 'col')
All inputs are finite; a program needn't handle non-finite values. No bound on the sum of `block_mask` on one device may be relied on, other than what follows from the above.
Results may differ from a plain program's by a relative error of at most 0.001.
Values may be sent and summed in bfloat16 or wider, within the bound.
A program may use at most 128 MiB of HBM per device.

v0:
```python
import jax
import jax.numpy as jnp
from jax import lax
from jax.sharding import PartitionSpec as P


def tables(count):
    index = jnp.arange(count, dtype=jnp.int32)
    phase = index[:, None] * index[None, :] % count
    angle = phase.astype(jnp.float32) * (2.0 * jnp.pi / count)
    return jnp.concatenate((jnp.cos(angle), jnp.sin(angle)), axis=1)


def transform(values, dim, inverse):
    moved = jnp.moveaxis(values, dim + 1, -1)
    count = moved.shape[-1]
    both = jnp.matmul(moved, tables(count), precision=lax.Precision.HIGHEST)
    with_cos = both[..., :count]
    with_sin = both[..., count:]
    if inverse:
        real_part = with_cos[0] - with_sin[1]
        imag_part = with_cos[1] + with_sin[0]
    else:
        real_part = with_cos[0] + with_sin[1]
        imag_part = with_cos[1] - with_sin[0]
    return jnp.moveaxis(jnp.stack((real_part, imag_part)), -1, dim + 1)


def transform_real(values):
    count = values.shape[-1]
    both = jnp.matmul(values, tables(count), precision=lax.Precision.HIGHEST)
    return jnp.stack((both[..., :count], -both[..., count:]))


def frequency(index, count):
    return jnp.where(index > count // 2, index - count, index)


def shards(density_matrix, block_mask, cell_group, electron_shape, ion_charge):
    rows, cols = density_matrix.shape
    brows, bcols = block_mask.shape
    blk = rows // brows
    keep = block_mask.astype(jnp.bfloat16)[:, None, :, None]
    masked = (density_matrix.reshape(brows, blk, bcols, blk) * keep).reshape(rows, cols)
    row_panel = lax.all_gather(masked, "col", axis=1, tiled=True)
    square = jnp.dot(
        row_panel,
        lax.all_gather(masked, "row", axis=0, tiled=True),
        preferred_element_type=jnp.float32,
    )
    keep_wide = block_mask.astype(jnp.float32)[:, None, :, None]
    update = (2.0 * masked.astype(jnp.float32) - square).reshape(brows, blk, bcols, blk) * keep_wide
    next_density = update.reshape(rows, cols).astype(jnp.bfloat16)
    nblocks = brows * lax.axis_size("row")
    row_global = lax.axis_index("row") * rows + jnp.arange(rows, dtype=jnp.int32)
    col_global = lax.axis_index("col") * cols + jnp.arange(cols, dtype=jnp.int32)
    on_diag = row_global[:, None] == col_global[None, :]
    diag_rows = jnp.sum(jnp.where(on_diag, square, 0.0), axis=1)
    local_pop = jnp.sum(diag_rows.reshape(brows, blk), axis=1)
    block_ids = lax.axis_index("row") * brows + jnp.arange(brows, dtype=jnp.int32)
    all_ids = jnp.arange(nblocks, dtype=jnp.int32)
    placed = jnp.sum(
        jnp.where(block_ids[:, None] == all_ids[None, :], local_pop[:, None], 0.0), axis=0
    )
    grid = electron_shape.shape[2]
    population, shape_sum = lax.psum((placed, jnp.sum(electron_shape)), ("row", "col"))
    weight = population * nblocks / jnp.sum(population)
    mean_shape = shape_sum / (grid * grid * grid)
    cell_weight = jnp.sum(
        jnp.where(cell_group[:, :, None] == all_ids[None, None, :], weight[None, None, :], 0.0),
        axis=2,
    )
    charge = cell_weight[:, :, None] * electron_shape / mean_shape - ion_charge
    values = transform_real(charge)
    values = lax.all_to_all(values, "col", split_axis=3, concat_axis=2, tiled=True)
    values = transform(values, 1, False)
    values = lax.all_to_all(values, "row", split_axis=2, concat_axis=1, tiled=True)
    values = transform(values, 0, False)
    span_second = values.shape[2]
    span_third = values.shape[3]
    first_idx = jnp.arange(grid, dtype=jnp.int32)
    second_idx = lax.axis_index("row") * span_second + jnp.arange(span_second, dtype=jnp.int32)
    third_idx = lax.axis_index("col") * span_third + jnp.arange(span_third, dtype=jnp.int32)
    freq_first = frequency(first_idx, grid)
    freq_second = frequency(second_idx, grid)
    freq_third = frequency(third_idx, grid)
    scale = 2.0 * jnp.pi / grid
    sq_first = (freq_first.astype(jnp.float32) * scale) ** 2
    sq_second = (freq_second.astype(jnp.float32) * scale) ** 2
    sq_third = (freq_third.astype(jnp.float32) * scale) ** 2
    ksq = sq_first[:, None, None] + sq_second[None, :, None] + sq_third[None, None, :]
    anchor = (
        (freq_first[:, None, None] == 0)
        & (freq_second[None, :, None] == 0)
        & (freq_third[None, None, :] == 0)
    )
    kappa = 8.0 / grid
    kernel = jnp.where(anchor, 0.0, 1.0 / (ksq + kappa * kappa))
    values = values * kernel[None]
    values = transform(values, 0, True)
    values = lax.all_to_all(values, "row", split_axis=1, concat_axis=2, tiled=True)
    values = transform(values, 1, True)
    values = lax.all_to_all(values, "col", split_axis=2, concat_axis=3, tiled=True)
    values = transform(values, 2, True)
    potential = values[0] / (grid * grid * grid)
    return (next_density, potential)


def solution(mesh):
    in_specs = (
        P("row", "col"),
        P("row", "col"),
        P("row", "col"),
        P("row", "col", None),
        P("row", "col", None),
    )
    out_specs = (P("row", "col"), P("row", "col", None))
    return jax.shard_map(shards, mesh=mesh, in_specs=in_specs, out_specs=out_specs, check_vma=False)
```

profile of v0, /device:TPU:9, one launch (start us, length us, event | category | flops | bytes accessed | tf_op | source)
XLA Modules:
  0.0 823.6 jit_solution(11220287858253598504)
XLA Ops:
  12.6 77.6 %all-gather.3.cloned.1.call-done = bf16[512,4096]{1,0:T(8,128)(2,1)} async-done(((bf16[512,1024]{1,0:T(8,128)(2,1)}), bf16[512,4096]{1,0:T(8,128)(2,1)}) %all-gather.3.cloned.1.call-update) | async-done | bytes 4194320 | tf_op jit(solution)/shard_map/all_gather | solution.py:45
  90.3 58.4 %all-gather.5.cloned.1.call-done = bf16[4096,1024]{1,0:T(8,128)(2,1)} async-done(((bf16[512,1024]{1,0:T(8,128)(2,1)}), bf16[4096,1024]{1,0:T(8,128)(2,1)}) %all-gather.5.cloned.1.call-update) | async-done | bytes 8388624 | tf_op jit(solution)/shard_map/all_gather | solution.py:48
  148.8 10.5 %select_reduce_fusion = (f32[512]{0:T(512)S(1)}, bf16[512,1024]{1,0:T(8,128)(2,1)}) fusion(s32[1024]{0:T(1024)S(1)} %iota_add_fusion, s32[512]{0:T(512)S(1)} %iota_add_fusion.1, f32[64,8,8,128]{3,2,1,0:T(8,128)S(1)} %bitcast.91, bf16[512,1024]{1,0:T(8,128)(2,1)S(1)} %copy-done, bf16[512,4096]{1,0:T(8,128)(2,1)} %all-gather.3.cloned.1.call-done, ...), kind=kOutput, calls=%fused_computation.38 | convolution fusion | flops 4299161088 | bytes 16785408 | tf_op jit(solution)/shard_map/dot_general | solution.py:46
  160.6 38.5 %all-reduce = (f32[]{:T(128)}, f32[32]{0:T(128)S(1)}) all-reduce(f32[]{:T(128)} %reduce_sum.59, f32[32]{0:T(128)S(1)} %select_reduce_fusion.2), channel_id=1, replica_groups=mesh['row'=8,'col'=4] {'row','col'}, use_global_device_ids=true, to_apply=%region_7.8 | all-reduce | flops 33 | bytes 264 | tf_op jit(solution)/shard_map/psum | solution.py:66
  227.7 96.3 %all_to_all.72 = f32[4,1,262144]{2,1,0:T(1,128)} all-to-all(f32[4,1,262144]{2,1,0:T(1,128)} %reshape.149), channel_id=1, replica_groups=mesh['row'=8,'col'=4] {'col'}, dimensions={0} | all-to-all | bytes 8388608 | tf_op jit(solution)/shard_map/all_to_all | solution.py:75
  324.5 15.5 %reduce = f32[4,262144]{1,0:T(4,128)} reduce(f32[4,1,262144]{2,1,0:T(1,128)} %all_to_all.72, f32[]{:T(128)} %broadcast.240), dimensions={1}, to_apply=%all_to_all.52.reduce_sub_computation | reduce | bytes 8388612 | tf_op jit(solution)/shard_map/all_to_all | solution.py:75
  340.0 9.3 %reshape.150 = f32[256,2,32,64]{3,2,1,0:T(8,128)} reshape(f32[4,262144]{1,0:T(4,128)} %reduce) | data formatting | bytes 8388608
  349.3 12.0 %copy.53 = f32[2,32,64,4,64]{2,3,4,1,0:T(4,128)} copy(f32[2,32,64,4,64]{2,1,0,4,3:T(8,128)} %bitcast.82) | data formatting | bytes 8388608 | tf_op jit(solution)/shard_map/all_to_all | solution.py:75
  369.8 10.1 %fusion.7 = f32[2,32,64,512]{3,2,1,0:T(8,128)S(1)} fusion(f32[2,32,256,64]{2,3,1,0:T(8,128)} %all_to_all.55, f32[256,256]{1,0:T(8,128)S(1)} %get-tuple-element.18, f32[256,256]{1,0:T(8,128)S(1)} %get-tuple-element.19), kind=kOutput, calls=%fused_computation.14 | convolution fusion | flops 6442582016 | bytes 13107200 | tf_op jit(solution)/shard_map/dot_general | solution.py:17
  383.2 9.1 %copy.33 = f32[2,32,256,64]{3,1,0,2:T(8,128)} copy(f32[2,32,256,64]{2,3,1,0:T(8,128)} %maximum_bitcast_fusion) | data formatting | bytes 8388608 | tf_op jit(solution)/shard_map/transpose | solution.py:26
  392.3 9.8 %reshape.151 = f32[8,1,131072]{2,1,0:T(1,128)} reshape(f32[256,2,32,64]{3,2,1,0:T(8,128)} %bitcast.79) | data formatting | bytes 8388608
  409.6 44.9 %all-to-all-done.1 = f32[8,1,131072]{2,1,0:T(1,128)} async-done(((f32[8,1,131072]{2,1,0:T(1,128)}), f32[8,1,131072]{2,1,0:T(1,128)}, u32[]{:S(2)}, u32[]{:S(2)}) %all-to-all-start.1) | async-done | bytes 4194336 | tf_op jit(solution)/shard_map/all_to_all | solution.py:77
  454.4 13.9 %reduce.1 = f32[8,131072]{1,0:T(8,128)} reduce(f32[8,1,131072]{2,1,0:T(1,128)} %all-to-all-done.1, f32[]{:T(128)} %broadcast.240), dimensions={1}, to_apply=%all_to_all.56.reduce_sub_computation | reduce | bytes 8388612 | tf_op jit(solution)/shard_map/all_to_all | solution.py:77
  477.0 13.1 %copy.35 = f32[2,8,32,32,64]{4,3,2,1,0:T(8,128)} copy(f32[2,8,32,32,64]{4,2,0,3,1:T(8,128)} %bitcast.84) | data formatting | bytes 8388608 | tf_op jit(solution)/shard_map/all_to_all | solution.py:77
  497.9 10.1 %fusion.5 = f32[2,32,64,512]{3,2,1,0:T(8,128)S(1)} fusion(f32[2,256,32,64]{1,3,2,0:T(8,128)} %copy.36, f32[256,256]{1,0:T(8,128)S(1)} %get-tuple-element.18, f32[256,256]{1,0:T(8,128)S(1)} %get-tuple-element.19), kind=kOutput, calls=%fused_computation.12 | convolution fusion | flops 6442582016 | bytes 13107200 | tf_op jit(solution)/shard_map/dot_general | solution.py:17
  528.7 9.8 %reshape.153 = f32[8,1,131072]{2,1,0:T(1,128)} reshape(f32[256,2,32,64]{3,2,1,0:T(8,128)} %bitcast.80) | data formatting | bytes 8388608
  538.5 56.0 %all_to_all.73 = f32[8,1,131072]{2,1,0:T(1,128)} all-to-all(f32[8,1,131072]{2,1,0:T(1,128)} %reshape.153), channel_id=1, replica_groups=mesh['row'=8,'col'=4] {'row'}, dimensions={0} | all-to-all | bytes 8388608 | tf_op jit(solution)/shard_map/all_to_all | solution.py:101
  594.5 13.7 %reduce.2 = f32[8,131072]{1,0:T(8,128)} reduce(f32[8,1,131072]{2,1,0:T(1,128)} %all_to_all.73, f32[]{:T(128)} %broadcast.240), dimensions={1}, to_apply=%all_to_all.60.reduce_sub_computation | reduce | bytes 8388612 | tf_op jit(solution)/shard_map/all_to_all | solution.py:101
  631.8 9.8 %fusion.3 = f32[2,32,64,512]{3,2,1,0:T(8,128)S(1)} fusion(f32[2,32,256,64]{2,3,1,0:T(8,128)} %copy.40, f32[256,256]{1,0:T(8,128)S(1)} %get-tuple-element.18, f32[256,256]{1,0:T(8,128)S(1)} %get-tuple-element.19), kind=kOutput, calls=%fused_computation.10 | convolution fusion | flops 6442582016 | bytes 13107200 | tf_op jit(solution)/shard_map/dot_general | solution.py:17
  662.5 97.5 %all_to_all.74 = f32[4,1,262144]{2,1,0:T(1,128)} all-to-all(f32[4,1,262144]{2,1,0:T(1,128)} %reshape.155), channel_id=1, replica_groups=mesh['row'=8,'col'=4] {'col'}, dimensions={0} | all-to-all | bytes 8388608 | tf_op jit(solution)/shard_map/all_to_all | solution.py:103
  760.0 15.5 %reduce.3 = f32[4,262144]{1,0:T(4,128)} reduce(f32[4,1,262144]{2,1,0:T(1,128)} %all_to_all.74, f32[]{:T(128)} %broadcast.240), dimensions={1}, to_apply=%all_to_all.64.reduce_sub_computation | reduce | bytes 8388612 | tf_op jit(solution)/shard_map/all_to_all | solution.py:103
  775.5 9.3 %reshape.156 = f32[256,2,32,64]{3,2,1,0:T(8,128)} reshape(f32[4,262144]{1,0:T(4,128)} %reduce.3) | data formatting | bytes 8388608
  784.8 12.0 %copy.52 = f32[2,32,4,64,64]{4,2,3,1,0:T(4,128)} copy(f32[2,32,4,64,64]{4,1,0,3,2:T(8,128)} %bitcast.88) | data formatting | bytes 8388608 | tf_op jit(solution)/shard_map/all_to_all | solution.py:103
  805.3 9.4 %fusion.20 = f32[2,32,64,512]{3,2,1,0:T(8,128)S(1)} fusion(f32[2,32,64,256]{3,2,1,0:T(8,128)} %all_to_all.67, f32[256,256]{1,0:T(8,128)S(1)} %get-tuple-element.18, f32[256,256]{1,0:T(8,128)S(1)} %get-tuple-element.19), kind=kOutput, calls=%fused_computation.43 | convolution fusion | flops 6442582016 | bytes 13107200 | tf_op jit(solution)/shard_map/dot_general | solution.py:17
  (59 shorter events, 146.3 us)
Async XLA Ops:
  7.2 83.1 %all-gather.3.cloned.1.call-start = ((), (), s32[]{:S(2)}) async-start(), calls=%async_computation.4 | async-start | bytes 5242880 | tf_op jit(solution)/shard_map/all_gather | solution.py:45
  8.2 3.3 copy-start.1
  10.7 137.9 %all-gather.5.cloned.1.call-start = ((), (), s32[]{:S(2)}) async-start(), calls=%async_computation.5 | async-start | bytes 9437184 | tf_op jit(solution)/shard_map/all_gather | solution.py:48
  11.5 137.4 %copy-start = (bf16[512,1024]{1,0:T(8,128)(2,1)S(1)}, bf16[512,1024]{1,0:T(8,128)(2,1)}, u32[]{:S(2)}) copy-start(bf16[512,1024]{1,0:T(8,128)(2,1)} %bitcast_multiply_fusion.1) | copy-start | bytes 3145732
  148.8 52.4 %copy-start.2 = (s32[32,64]{1,0:T(8,128)S(1)}, s32[32,64]{1,0:T(8,128)}, u32[]{:S(2)}) copy-start(s32[32,64]{1,0:T(8,128)} %param.7) | copy-start | bytes 24580
  402.2 52.3 %all-to-all-start.1 = ((f32[8,1,131072]{2,1,0:T(1,128)}), f32[8,1,131072]{2,1,0:T(1,128)}, u32[]{:S(2)}, u32[]{:S(2)}) async-start(f32[8,1,131072]{2,1,0:T(1,128)} %reshape.151), calls=%async_computation.1 | async-start | bytes 8388608 | tf_op jit(solution)/shard_map/all_to_all | solution.py:77
Sparse Core Ops, SparseCore 0:
  10.8 79.3 all-gather.2
  92.7 55.8 all-gather.4
where the time goes:
time: 840 us; the launch traced here: 824 us
  blocking collectives  288 us (34%)
  local copies, waits for them, and re-layouts  187 us (22%)
  waiting for transfers between devices  182 us (22%)
  other arithmetic  81.4 us (10%)
  matrix products  63.1 us (8%)
  between operations  15.4 us (2%)
    all_to_all x1, blocking collectives, shards(): lax.all_to_all(values, 'col', split_axis=2, concat_axis=3, tiled=True)  97.5 us
    all_to_all x1, blocking collectives, shards(): lax.all_to_all(values, 'col', split_axis=3, concat_axis=2, tiled=True)  96.3 us
    all_gather x1, waiting for transfers between devices, shards(): row_panel = lax.all_gather(masked, 'col', axis=1, tiled=True)  77.6 us
    unnamed x14, local copies, waits for them, and re-layouts  72.8 us
    all_gather x1, waiting for transfers between devices, shards(): lax.all_gather(masked, 'row', axis=0, tiled=True)  58.4 us
    all_to_all x1, blocking collectives, shards(): lax.all_to_all(values, 'row', split_axis=1, concat_axis=2, tiled=True)  56 us
    dot_general x5, matrix products, transform(): both = jnp.matmul(moved, tables(count), precision=lax.Precision.HIGHEST)  46.9 us
    all_to_all x1, waiting for transfers between devices, shards(): lax.all_to_all(values, 'row', split_axis=2, concat_axis=1, tiled=True)  44.9 us
  transfers between devices with their start and end apart: 3, of which 3 were waited for; matrix products, arithmetic and copies ran while one was open for 0% of the time, Pallas kernels for 0%

commit v1 on v0

v1 whole, which is shorter than its diff:
```python
import functools

import jax
import jax.numpy as jnp
import ml_dtypes
import numpy as np
from jax import lax
from jax.experimental import pallas as pl
from jax.experimental.pallas import tpu as pltpu
from jax.sharding import PartitionSpec as P

MESH = pl.DeviceIdType.MESH
F32 = jnp.float32
BF16 = jnp.bfloat16
NN = (((1,), (0,)), ((), ()))
NT = (((1,), (1,)), ((), ()))
TN = (((0,), (0,)), ((), ()))


def fourier_basis(count):
    half = count // 2
    place = np.arange(count)
    rows = np.zeros((count, count))
    rows[0] = 1.0 / np.sqrt(count)
    for f in range(1, half):
        rows[f] = np.sqrt(2.0 / count) * np.cos(2.0 * np.pi * (f * place % count) / count)
        rows[half + f] = np.sqrt(2.0 / count) * np.sin(2.0 * np.pi * (f * place % count) / count)
    rows[half] = np.where(place % 2 == 0, 1.0, -1.0) / np.sqrt(count)
    return rows


def split(table):
    high = table.astype(np.float32).astype(ml_dtypes.bfloat16)
    low = (table - high.astype(np.float64)).astype(np.float32).astype(ml_dtypes.bfloat16)
    return np.stack((high, low))


def make_tables(grid, nrow, ncol):
    span_m, span_n = grid // nrow, grid // ncol
    per = 128 // span_n
    groups = span_m // per
    basis = fourier_basis(grid)
    pair = np.zeros((ncol, 128, per * grid))
    for i in range(ncol):
        for u in range(per):
            pair[i, u * span_n:(u + 1) * span_n, u * grid:(u + 1) * grid] = basis[:, i * span_n:(i + 1) * span_n].T
    order = np.arange(grid).reshape(nrow, groups, per).transpose(0, 2, 1).reshape(-1)
    first = basis[:, order]
    return split(basis), split(pair), split(first), split(first.T)


def halves(x):
    high = x.astype(BF16)
    return high, (x - high.astype(F32)).astype(BF16)


def dot_right(x, high, low, dims):
    xh, xl = halves(x)
    dot = functools.partial(lax.dot_general, dimension_numbers=dims, preferred_element_type=F32)
    return dot(xh, high) + (dot(xl, high) + dot(xh, low))


def dot_left(high, low, x, dims):
    xh, xl = halves(x)
    dot = functools.partial(lax.dot_general, dimension_numbers=dims, preferred_element_type=F32)
    return dot(high, xh) + (dot(high, xl) + dot(low, xh))


def encode(x, value_ref, scale_ref):
    top = jnp.max(jnp.abs(x), axis=1, keepdims=True)
    unit = jnp.maximum(top, 1e-30) * (1.0 / 32760.0)
    value_ref[...] = jnp.round(x / unit).astype(jnp.int32).astype(jnp.int16)
    scale_ref[...] = unit[:, 0, :]


def decode(value, scale):
    return value.astype(jnp.int32).astype(F32) * scale[:, None, :]


def field_kernel(nrow, ncol, grid, wide,
                 charge_ref, basis_ref, pair_ref, first_ref, firstt_ref, out_ref,
                 turn, back, *bufs):
    nb = 1 if wide else 2
    stages = [bufs[k * 2 * nb:(k + 1) * 2 * nb] for k in range(4)]
    sems = bufs[8 * nb:]
    my_row, my_col = lax.axis_index("row"), lax.axis_index("col")
    span_m, span_n = grid // nrow, grid // ncol
    per = 128 // span_n
    groups = span_m // per
    thin = span_n // nrow
    barrier = pltpu.get_barrier_semaphore()

    @pl.loop(1, ncol)
    def _(t):
        pl.semaphore_signal(barrier, inc=1, device_id={"col": (my_col + t) % ncol}, device_id_type=MESH)

    @pl.loop(1, nrow)
    def _(t):
        pl.semaphore_signal(barrier, inc=1, device_id={"row": (my_row + t) % nrow}, device_id_type=MESH)

    pl.semaphore_wait(barrier, ncol - 1 + nrow - 1)

    def copies(stage, axis, me, dest, src):
        res = []
        for b in range(nb):
            send, recv = stages[stage][b], stages[stage][nb + b]
            ssem, rsem = sems[stage * 2], sems[stage * 2 + 1]
            res.append(pltpu.make_async_remote_copy(
                src_ref=send.at[dest], dst_ref=recv.at[me],
                send_sem=ssem.at[b, dest], recv_sem=rsem.at[b, src],
                device_id={axis: dest}, device_id_type=MESH))
        return res

    def put(stage, where, rows, x):
        if wide:
            stages[stage][0][where, rows] = x
        else:
            encode(x, stages[stage][0].at[where, rows], stages[stage][1].at[where, rows])

    def get(stage, src, rows):
        if wide:
            return stages[stage][1][src, rows]
        return decode(stages[stage][2][src, rows], stages[stage][3][src, rows])

    def finish(stage, axis, me, count):
        for b in range(nb):
            stages[stage][nb + b][me] = stages[stage][b][me]

        @pl.loop(1, count)
        def _(t):
            src = (me + count - t) % count
            for c in copies(stage, axis, me, src, src):
                c.wait_recv()

        @pl.loop(1, count)
        def _(t):
            dest = (me + t) % count
            for c in copies(stage, axis, me, dest, dest):
                c.wait_send()

    @pl.loop(0, groups)
    def _(k):
        block = charge_ref[pl.ds(pl.multiple_of(k * 128, 128), 128), :]
        turn[k] = dot_left(basis_ref[0], basis_ref[1], block, NT)

    @pl.loop(0, ncol)
    def _(t):
        dest = (my_col + 1 + t) % ncol

        @pl.loop(0, span_n // 16)
        def _(q):
            x = turn[:, pl.ds(pl.multiple_of(dest * span_n + q * 16, 16), 16), :]
            put(0, dest, pl.ds(pl.multiple_of(q * 16, 16), 16), jnp.swapaxes(x, 0, 1))

        @pl.when(t < ncol - 1)
        def _():
            for c in copies(0, "col", my_col, dest, my_col):
                c.start()

    finish(0, "col", my_col, ncol)

    @pl.loop(0, nrow)
    def _(t):
        dest = (my_row + 1 + t) % nrow
        rows = pl.ds(dest * thin, thin)
        acc = jnp.zeros((thin * groups, per * grid), F32)
        for i in range(ncol):
            x = get(0, i, rows).reshape(thin * groups, 128)
            acc = acc + dot_right(x, pair_ref[0, i], pair_ref[1, i], NN)
        parts = [acc[:, u * grid:(u + 1) * grid].reshape(thin, groups, grid) for u in range(per)]
        put(1, dest, slice(None), jnp.concatenate(parts, axis=1))

        @pl.when(t < nrow - 1)
        def _():
            for c in copies(1, "row", my_row, dest, my_row):
                c.start()

    finish(1, "row", my_row, nrow)

    unit = 2.0 * np.pi / grid
    kappa = 8.0 / grid
    half = grid // 2

    def squared(index):
        f = jnp.where(index > half, index - half, index).astype(F32) * unit
        return f * f

    ia = lax.broadcasted_iota(jnp.int32, (grid, grid), 0)
    ib = lax.broadcasted_iota(jnp.int32, (grid, grid), 1)

    @pl.loop(0, thin)
    def _(k):
        x = jnp.concatenate([get(1, s, pl.ds(k, 1))[0] for s in range(nrow)], axis=0)
        y = dot_left(first_ref[0], first_ref[1], x, NN)
        third = my_col * span_n + my_row * thin + k
        ksq = squared(ia) + squared(ib) + squared(third)
        gain = jnp.where((ia + ib + third) == 0, 0.0, (kappa * kappa) / (ksq + kappa * kappa))
        z = dot_left(firstt_ref[0], firstt_ref[1], y * gain, NN)
        for s in range(nrow):
            put(2, s, pl.ds(k, 1), z[None, s * span_m:(s + 1) * span_m])

    @pl.loop(1, nrow)
    def _(t):
        for c in copies(2, "row", my_row, (my_row + t) % nrow, my_row):
            c.start()

    finish(2, "row", my_row, nrow)

    @pl.loop(0, ncol)
    def _(t):
        dest = (my_col + 1 + t) % ncol

        @pl.loop(0, nrow)
        def _(s):
            x = get(2, s, slice(None))
            acc = jnp.zeros((thin * groups, 128), F32)
            for u in range(per):
                xu = x[:, u * groups:(u + 1) * groups].reshape(thin * groups, grid)
                cut = slice(u * grid, (u + 1) * grid)
                acc = acc + dot_right(xu, pair_ref[0, dest, :, cut], pair_ref[1, dest, :, cut], NT)
            put(3, dest, pl.ds(s * thin, thin), acc.reshape(thin, groups, 128))

        @pl.when(t < ncol - 1)
        def _():
            for c in copies(3, "col", my_col, dest, my_col):
                c.start()

    finish(3, "col", my_col, ncol)

    @pl.loop(0, ncol)
    def _(i):
        @pl.loop(0, span_n // 16)
        def _(q):
            rows = pl.ds(pl.multiple_of(q * 16, 16), 16)
            x = get(3, i, rows)
            back[:, pl.ds(pl.multiple_of(i * span_n + q * 16, 16), 16), :] = jnp.swapaxes(x, 0, 1)

    @pl.loop(0, groups)
    def _(k):
        x = dot_right(back[k], basis_ref[0], basis_ref[1], TN)
        out_ref[pl.ds(pl.multiple_of(k * 128, 128), 128), :] = x * (1.0 / (kappa * kappa))


def solve(charge, nrow, ncol, grid, wide):
    span_m, span_n = grid // nrow, grid // ncol
    per = 128 // span_n
    groups = span_m // per
    thin = span_n // nrow
    tables = [jnp.asarray(t) for t in make_tables(grid, nrow, ncol)]
    scratch = [pltpu.VMEM((groups, grid, 128), F32), pltpu.VMEM((groups, grid, 128), F32)]
    col_shape, row_shape = (ncol, span_n, groups, 128), (nrow, thin, span_m, grid)
    for shape in (col_shape, row_shape, row_shape, col_shape):
        for _ in range(2):
            if wide:
                scratch.append(pltpu.VMEM(shape, F32))
            else:
                scratch.append(pltpu.VMEM(shape, jnp.int16))
                scratch.append(pltpu.VMEM(shape[:2] + shape[3:], F32))
    for count in (ncol, nrow, nrow, ncol):
        for _ in range(2):
            scratch.append(pltpu.SemaphoreType.DMA((1 if wide else 2, count)))
    return pl.pallas_call(
        functools.partial(field_kernel, nrow, ncol, grid, wide),
        out_shape=jax.ShapeDtypeStruct((span_m * span_n, grid), F32),
        in_specs=[pl.BlockSpec(memory_space=pltpu.VMEM)] * 5,
        out_specs=pl.BlockSpec(memory_space=pltpu.VMEM),
        scratch_shapes=scratch,
        compiler_params=pltpu.CompilerParams(
            collective_id=0, has_side_effects=True, vmem_limit_bytes=56 * 1024 * 1024),
    )(charge, *tables)


def shards(density_matrix, block_mask, cell_group, electron_shape, ion_charge):
    rows, cols = density_matrix.shape
    brows, bcols = block_mask.shape
    blk = rows // brows
    keep = block_mask.astype(BF16)[:, None, :, None]
    masked = (density_matrix.reshape(brows, blk, bcols, blk) * keep).reshape(rows, cols)
    row_panel = lax.all_gather(masked, "col", axis=1, tiled=True)
    square = jnp.dot(
        row_panel,
        lax.all_gather(masked, "row", axis=0, tiled=True),
        preferred_element_type=F32,
    )
    keep_wide = block_mask.astype(F32)[:, None, :, None]
    update = (2.0 * masked.astype(F32) - square).reshape(brows, blk, bcols, blk) * keep_wide
    next_density = update.reshape(rows, cols).astype(BF16)
    nrow, ncol = lax.axis_size("row"), lax.axis_size("col")
    nblocks = brows * nrow
    row_global = lax.axis_index("row") * rows + jnp.arange(rows, dtype=jnp.int32)
    col_global = lax.axis_index("col") * cols + jnp.arange(cols, dtype=jnp.int32)
    on_diag = row_global[:, None] == col_global[None, :]
    diag_rows = jnp.sum(jnp.where(on_diag, square, 0.0), axis=1)
    local_pop = jnp.sum(diag_rows.reshape(brows, blk), axis=1)
    block_ids = lax.axis_index("row") * brows + jnp.arange(brows, dtype=jnp.int32)
    all_ids = jnp.arange(nblocks, dtype=jnp.int32)
    placed = jnp.sum(
        jnp.where(block_ids[:, None] == all_ids[None, :], local_pop[:, None], 0.0), axis=0
    )
    grid = electron_shape.shape[2]
    population, shape_sum = lax.psum((placed, jnp.sum(electron_shape)), ("row", "col"))
    weight = population * nblocks / jnp.sum(population)
    mean_shape = shape_sum / (grid * grid * grid)
    cell_weight = jnp.sum(
        jnp.where(cell_group[:, :, None] == all_ids[None, None, :], weight[None, None, :], 0.0),
        axis=2,
    )
    charge = cell_weight[:, :, None] * electron_shape / mean_shape - ion_charge
    potential = solve(charge.reshape(-1, grid), nrow, ncol, grid, WIDE)
    return next_density, potential.reshape(electron_shape.shape)


WIDE = False


def solution(mesh):
    in_specs = (
        P("row", "col"),
        P("row", "col"),
        P("row", "col"),
        P("row", "col", None),
        P("row", "col", None),
    )
    out_specs = (P("row", "col"), P("row", "col", None))
    return jax.shard_map(shards, mesh=mesh, in_specs=in_specs, out_specs=out_specs, check_vma=False)
```

time: 840 us -> 322 us (0.38); the launches traced: 824 us -> 321 us
  blocking collectives: 288 us -> 38.5 us
  local copies, waits for them, and re-layouts: 187 us -> 3.56 us
  Pallas kernels: 0 us -> 108 us
  other arithmetic: 81.4 us -> 9.48 us
  matrix products: 63.1 us -> 10.5 us
  waiting for transfers between devices: 182 us -> 137 us
    all_to_all x3 -> x0, blocking collectives: 250 us -> none  [the longest x1 97.5 us: shards(): lax.all_to_all(values, 'col', split_axis=2, concat_axis=3, tiled=True)]
    pallas_call x0 -> x1, Pallas kernels: none -> 108 us  [solve(): pl.pallas_call(functools.partial(field_kernel, nrow, ncol, grid, wide), o...]
    all_to_all x9 -> x0, local copies, waits for them, and re-layouts: 77.3 us -> none  [the longest x3 21.1 us: shards(): lax.all_to_all(values, 'col', split_axis=3, concat_axis=2, tiled=True)]
    unnamed x14 -> x7, local copies, waits for them, and re-layouts: 72.8 us -> 3.15 us
    all_to_all x4 -> x0, other arithmetic: 58.5 us -> none  [the longest x1 15.5 us: shards(): lax.all_to_all(values, 'col', split_axis=2, concat_axis=3, tiled=True)]
    dot_general x6 -> x0, matrix products: 52.6 us -> none  [the longest x5 46.9 us: transform(): both = jnp.matmul(moved, tables(count), precision=lax.Precision.HIGHEST)]
    all_to_all x1 -> x0, waiting for transfers between devices: 44.9 us -> none  [shards(): lax.all_to_all(values, 'row', split_axis=2, concat_axis=1, tiled=True)]
    transpose x3 -> x0, local copies, waits for them, and re-layouts: 27.4 us -> none  [transform(): return jnp.moveaxis(jnp.stack((real_part, imag_part)), -1, dim + 1)]
  transfers between devices with their start and end apart: 3 -> 2, of which waited for: 3 -> 2; matrix products, arithmetic and copies ran while one was open for 0% -> 0% of each run, Pallas kernels for 0% -> 0%
where the time goes in v1:
time: 322 us; the launch traced here: 321 us
  waiting for transfers between devices  137 us (43%)
  Pallas kernels  108 us (34%)
  blocking collectives  38.5 us (12%)
  between operations  14.8 us (5%)
  matrix products  10.5 us (3%)
  other arithmetic  9.48 us (3%)
  local copies, waits for them, and re-layouts  3.56 us (1%)
    pallas_call x1, Pallas kernels, solve(): pl.pallas_call(functools.partial(field_kernel, nrow, ncol, grid, wide), o...  108 us
    all_gather x1, waiting for transfers between devices, shards(): row_panel = lax.all_gather(masked, 'col', axis=1, tiled=True)  77.6 us
    all_gather x1, waiting for transfers between devices, shards(): lax.all_gather(masked, 'row', axis=0, tiled=True)  58.4 us
    psum x1, blocking collectives, shards(): lax.psum((placed, jnp.sum(electron_shape)), ('row', 'col'))  38.5 us
    dot_general x1, matrix products, shards(): jnp.dot(row_panel, lax.all_gather(masked, 'row', axis=0, tiled=True), pre...  10.5 us
  transfers between devices with their start and end apart: 2, of which 2 were waited for; matrix products, arithmetic and copies ran while one was open for 0% of the time, Pallas kernels for 0%

profile of v1, /device:TPU:9, one launch (start us, length us, event | category | flops | bytes accessed | tf_op | source)
XLA Modules:
  0.0 321.2 jit_solution(6510362293968959128)
XLA Ops:
  7.2 0.0 all-gather.3.cloned.1.call-start
  7.2 0.8 fusion.1
  8.0 0.2 mul.51
  8.2 0.0 copy-start.1
  8.2 2.5 bitcast_multiply_fusion.1
  10.7 0.0 all-gather.3.cloned.1.call-update
  10.7 0.0 all-gather.5.cloned.1.call-start
  10.8 0.7 all-gather.5.cloned.1.call-update
  11.5 0.0 copy-start
  11.5 1.1 reduce_sum.59
  12.6 77.6 %all-gather.3.cloned.1.call-done = bf16[512,4096]{1,0:T(8,128)(2,1)} async-done(((bf16[512,1024]{1,0:T(8,128)(2,1)}), bf16[512,4096]{1,0:T(8,128)(2,1)}) %all-gather.3.cloned.1.call-update) | async-done | bytes 4194320 | tf_op jit(solution)/shard_map/all_gather | solution.py:279
  90.3 58.4 %all-gather.5.cloned.1.call-done = bf16[4096,1024]{1,0:T(8,128)(2,1)} async-done(((bf16[512,1024]{1,0:T(8,128)(2,1)}), bf16[4096,1024]{1,0:T(8,128)(2,1)}) %all-gather.5.cloned.1.call-update) | async-done | bytes 8388624 | tf_op jit(solution)/shard_map/all_gather | solution.py:282
  148.6 0.2 mul.56
  148.8 0.0 copy-start.2
  148.8 10.5 %select_reduce_fusion = (f32[512]{0:T(512)S(1)}, bf16[512,1024]{1,0:T(8,128)(2,1)}) fusion(s32[1024]{0:T(1024)S(1)} %iota_add_fusion, s32[512]{0:T(512)S(1)} %iota_add_fusion.1, f32[64,8,8,128]{3,2,1,0:T(8,128)S(1)} %bitcast.19, bf16[512,1024]{1,0:T(8,128)(2,1)S(1)} %copy-done, bf16[512,4096]{1,0:T(8,128)(2,1)} %all-gather.3.cloned.1.call-done, ...), kind=kOutput, calls=%fused_computation.3 | convolution fusion | flops 4299161088 | bytes 16785408 | tf_op jit(solution)/shard_map/dot_general | solution.py:280
  159.4 0.1 bitcast_reduce_fusion
  159.5 0.1 select_reduce_fusion.2
  159.6 38.5 %all-reduce = (f32[]{:T(128)}, f32[32]{0:T(128)S(1)}) all-reduce(f32[]{:T(128)} %reduce_sum.59, f32[32]{0:T(128)S(1)} %select_reduce_fusion.2), channel_id=1, replica_groups=mesh['row'=8,'col'=4] {'row','col'}, use_global_device_ids=true, to_apply=%region_7.8 | all-reduce | flops 33 | bytes 264 | tf_op jit(solution)/shard_map/psum | solution.py:301
  198.1 0.7 reduce_sum.57
  198.7 0.7 multiply_divide_fusion
  199.4 0.2 select_reduce_fusion.1
  200.3 3.3 %divide_subtract_fusion = f32[32,64,256]{2,1,0:T(8,128)} fusion(f32[32,64,256]{2,1,0:T(8,128)} %param.13, f32[32,64,256]{2,1,0:T(8,128)S(1)} %copy-done.1, f32[]{:T(128)S(6)} %div.17, f32[32,64]{1,0:T(8,128)S(1)} %select_reduce_fusion.1), kind=kLoop, calls=%fused_computation.2 | loop fusion | flops 1572864 | bytes 6299652 | tf_op jit(solution)/shard_map/sub | solution.py:308
  203.6 107.6 %shard_map.104 = f32[2048,256]{1,0:T(8,128)} custom-call(f32[2048,256]{1,0:T(8,128)} %bitcast.16, bf16[2,256,256]{2,1,0:T(8,128)(2,1)} %constant.32.clone.basis_ref, bf16[2,4,128,512]{3,2,1,0:T(8,128)(2,1)} %constant.33.clone.pair_ref, bf16[2,256,256]{2,1,0:T(8,128)(2,1)} %constant.34.clone.first_ref, bf16[2,256,256]{2,1,0:T(8,128)(2,1)} %constant.35.clone.firstt_ref), custom_call_target="tpu_custom_call" | custom-call | tf_op jit(solution)/shard_map/pallas_call | solution.py:262
  311.2 3.1 copy.16
  (6 shorter events, 0.0 us)
Async XLA Ops:
  7.2 83.1 %all-gather.3.cloned.1.call-start = ((), (), s32[]{:S(2)}) async-start(), calls=%async_computation | async-start | bytes 5242880 | tf_op jit(solution)/shard_map/all_gather | solution.py:279
  8.2 3.3 %copy-start.1 = (f32[32,64,256]{2,1,0:T(8,128)S(1)}, f32[32,64,256]{2,1,0:T(8,128)}, u32[]{:S(2)}) copy-start(f32[32,64,256]{2,1,0:T(8,128)} %param.12) | copy-start | bytes 6291460
  10.7 137.9 %all-gather.5.cloned.1.call-start = ((), (), s32[]{:S(2)}) async-start(), calls=%async_computation.1 | async-start | bytes 9437184 | tf_op jit(solution)/shard_map/all_gather | solution.py:282
  11.5 137.4 %copy-start = (bf16[512,1024]{1,0:T(8,128)(2,1)S(1)}, bf16[512,1024]{1,0:T(8,128)(2,1)}, u32[]{:S(2)}) copy-start(bf16[512,1024]{1,0:T(8,128)(2,1)} %bitcast_multiply_fusion.1) | copy-start | bytes 3145732
  148.8 50.6 %copy-start.2 = (s32[32,64]{1,0:T(8,128)S(1)}, s32[32,64]{1,0:T(8,128)}, u32[]{:S(2)}) copy-start(s32[32,64]{1,0:T(8,128)} %param.11) | copy-start | bytes 24580
Sparse Core Ops, SparseCore 0:
  10.8 79.3 all-gather.2
  92.7 55.8 all-gather.4

commit v2 on v1

--- a/solution.py
+++ b/solution.py
@@ -270,35 +270,152 @@
     )(charge, *tables)
 
 
+def trace_kernel(nrow, ncol, blk, a_ref, part_ref, out_ref, got, acc, mine, row_in, col_in,
+                 tile_send, tile_recv, row_send, row_recv, col_send, col_recv):
+    my_row, my_col = lax.axis_index("row"), lax.axis_index("col")
+    rows = a_ref.shape[0]
+    ratio = nrow // ncol
+    inner = rows // blk
+    barrier = pltpu.get_barrier_semaphore()
+
+    def place(h):
+        other = ratio * my_col + h
+        upper = (my_row < other) & ((my_row + other) % 2 == 0)
+        lower = (my_row > other) & ((my_row + other) % 2 == 1)
+        return other, upper | lower, my_row == other
+
+    @pl.loop(1, ncol)
+    def _(t):
+        pl.semaphore_signal(barrier, inc=1, device_id={"col": (my_col + t) % ncol}, device_id_type=MESH)
+
+    @pl.loop(1, nrow)
+    def _(t):
+        pl.semaphore_signal(barrier, inc=1, device_id={"row": (my_row + t) % nrow}, device_id_type=MESH)
+
+    expected = ncol - 1 + nrow - 1
+    for h in range(ratio):
+        other, sends, same = place(h)
+        expected = expected + jnp.where(sends, 1, 0)
+
+        @pl.when(jnp.logical_not(sends | same))
+        def _():
+            pl.semaphore_signal(barrier, inc=1, device_id={"row": other, "col": my_row // ratio},
+                                device_id_type=MESH)
+
+    pl.semaphore_wait(barrier, expected)
+
+    def tile_copy(h, other, slot):
+        return pltpu.make_async_remote_copy(
+            src_ref=a_ref.at[:, h * rows:(h + 1) * rows], dst_ref=got.at[slot],
+            send_sem=tile_send.at[h], recv_sem=tile_recv.at[slot],
+            device_id={"row": other, "col": my_row // ratio}, device_id_type=MESH)
+
+    for h in range(ratio):
+        other, sends, same = place(h)
+
+        @pl.when(sends)
+        def _():
+            tile_copy(h, other, my_row % ratio).start()
+
+    acc[...] = part_ref[...]
+    lane = lax.broadcasted_iota(jnp.int32, acc.shape, 1)
+    line = lax.broadcasted_iota(jnp.int32, acc.shape, 0)
+    eye = (lax.broadcasted_iota(jnp.int32, (blk, blk), 0)
+           == lax.broadcasted_iota(jnp.int32, (blk, blk), 1))
+    for h in range(ratio):
+        other, sends, same = place(h)
+
+        @pl.when(same)
+        def _():
+            got[h] = a_ref[:, h * rows:(h + 1) * rows]
+
+        @pl.when(jnp.logical_not(sends | same))
+        def _():
+            tile_copy(h, other, h).wait_recv()
+
+        @pl.when(jnp.logical_not(sends))
+        def _():
+            for g in range(inner):
+                for k in range(inner):
+                    prod = jnp.dot(
+                        a_ref[g * blk:(g + 1) * blk, h * rows + k * blk:h * rows + (k + 1) * blk],
+                        got[h, k * blk:(k + 1) * blk, g * blk:(g + 1) * blk],
+                        preferred_element_type=F32)
+                    value = jnp.sum(jnp.where(eye, prod, 0.0))
+                    here = (line == 0) & (lane == my_row * inner + g)
+                    there = (line == 0) & (lane == other * inner + k) & (my_row != other)
+                    acc[...] += jnp.where(here, value, 0.0) + jnp.where(there, value, 0.0)
+
+    for h in range(ratio):
+        other, sends, same = place(h)
+
+        @pl.when(sends)
+        def _():
+            tile_copy(h, other, my_row % ratio).wait_send()
+
+    def total(axis, me, count, src_ref, slots, send, recv, dst_ref):
+        def one(t, who, slot):
+            return pltpu.make_async_remote_copy(
+                src_ref=src_ref, dst_ref=slots.at[me], send_sem=send.at[t], recv_sem=recv.at[slot],
+                device_id={axis: who}, device_id_type=MESH)
+
+        @pl.loop(1, count)
+        def _(t):
+            one(t, (me + t) % count, me).start()
+
+        slots[me] = src_ref[...]
+
+        @pl.loop(1, count)
+        def _(t):
+            one(t, (me + t) % count, (me + t) % count).wait_recv()
+
+        dst_ref[...] = jnp.sum(slots[...], axis=0)
+
+        @pl.loop(1, count)
+        def _(t):
+            one(t, (me + t) % count, me).wait_send()
+
+    total("row", my_row, nrow, acc, row_in, row_send, row_recv, mine)
+    total("col", my_col, ncol, mine, col_in, col_send, col_recv, out_ref)
+
+
+def traces(masked, part, nrow, ncol, blk):
+    rows, cols = masked.shape
+    ratio = nrow // ncol
+    small = (8, 128)
+    dma = pltpu.SemaphoreType.DMA
+    return pl.pallas_call(
+        functools.partial(trace_kernel, nrow, ncol, blk),
+        out_shape=jax.ShapeDtypeStruct(small, F32),
+        in_specs=[pl.BlockSpec(memory_space=pltpu.VMEM)] * 2,
+        out_specs=pl.BlockSpec(memory_space=pltpu.VMEM),
+        scratch_shapes=[
+            pltpu.VMEM((ratio, rows, rows), BF16), pltpu.VMEM(small, F32), pltpu.VMEM(small, F32),
+            pltpu.VMEM((nrow,) + small, F32), pltpu.VMEM((ncol,) + small, F32),
+            dma((ratio,)), dma((ratio,)), dma((nrow,)), dma((nrow,)), dma((ncol,)), dma((ncol,)),
+        ],
+        compiler_params=pltpu.CompilerParams(
+            collective_id=1, has_side_effects=True, vmem_limit_bytes=16 * 1024 * 1024),
+    )(masked, part)
+
+
 def shards(density_matrix, block_mask, cell_group, electron_shape, ion_charge):
     rows, cols = density_matrix.shape
     brows, bcols = block_mask.shape
     blk = rows // brows
+    grid = electron_shape.shape[2]
+    nrow, ncol = lax.axis_size("row"), lax.axis_size("col")
+    nblocks = brows * nrow
     keep = block_mask.astype(BF16)[:, None, :, None]
     masked = (density_matrix.reshape(brows, blk, bcols, blk) * keep).reshape(rows, cols)
     row_panel = lax.all_gather(masked, "col", axis=1, tiled=True)
-    square = jnp.dot(
-        row_panel,
-        lax.all_gather(masked, "row", axis=0, tiled=True),
-        preferred_element_type=F32,
-    )
-    keep_wide = block_mask.astype(F32)[:, None, :, None]
-    update = (2.0 * masked.astype(F32) - square).reshape(brows, blk, bcols, blk) * keep_wide
-    next_density = update.reshape(rows, cols).astype(BF16)
-    nrow, ncol = lax.axis_size("row"), lax.axis_size("col")
-    nblocks = brows * nrow
-    row_global = lax.axis_index("row") * rows + jnp.arange(rows, dtype=jnp.int32)
-    col_global = lax.axis_index("col") * cols + jnp.arange(cols, dtype=jnp.int32)
-    on_diag = row_global[:, None] == col_global[None, :]
-    diag_rows = jnp.sum(jnp.where(on_diag, square, 0.0), axis=1)
-    local_pop = jnp.sum(diag_rows.reshape(brows, blk), axis=1)
-    block_ids = lax.axis_index("row") * brows + jnp.arange(brows, dtype=jnp.int32)
+    col_panel = lax.all_gather(masked, "row", axis=0, tiled=True)
+    line = jnp.arange(8, dtype=jnp.int32)[:, None]
+    lane = jnp.arange(128, dtype=jnp.int32)[None, :]
+    part = jnp.where((line == 1) & (lane == 0), jnp.sum(electron_shape), 0.0)
+    sums = traces(masked, part, nrow, ncol, blk)
+    population, shape_sum = sums[0, :nblocks], sums[1, 0]
     all_ids = jnp.arange(nblocks, dtype=jnp.int32)
-    placed = jnp.sum(
-        jnp.where(block_ids[:, None] == all_ids[None, :], local_pop[:, None], 0.0), axis=0
-    )
-    grid = electron_shape.shape[2]
-    population, shape_sum = lax.psum((placed, jnp.sum(electron_shape)), ("row", "col"))
     weight = population * nblocks / jnp.sum(population)
     mean_shape = shape_sum / (grid * grid * grid)
     cell_weight = jnp.sum(
@@ -307,6 +424,10 @@
     )
     charge = cell_weight[:, :, None] * electron_shape / mean_shape - ion_charge
     potential = solve(charge.reshape(-1, grid), nrow, ncol, grid, WIDE)
+    square = jnp.dot(row_panel, col_panel, preferred_element_type=F32)
+    keep_wide = block_mask.astype(F32)[:, None, :, None]
+    update = (2.0 * masked.astype(F32) - square).reshape(brows, blk, bcols, blk) * keep_wide
+    next_density = update.reshape(rows, cols).astype(BF16)
     return next_density, potential.reshape(electron_shape.shape)
 
 

time: 322 us -> 231 us (0.72)
  waiting for transfers between devices: 137 us -> 0.75 us
  Pallas kernels: 108 us -> 192 us
  blocking collectives: 38.5 us -> 0 us
    all_gather x1, waiting for transfers between devices: 77.6 us -> 0.02 us  [shards(): row_panel = lax.all_gather(masked, 'col', axis=1, tiled=True)]
    pallas_call x0 -> x1, Pallas kernels: none -> 68 us  [traces(): pl.pallas_call(functools.partial(trace_kernel, nrow, ncol, blk), out_shap...]
    all_gather x1, waiting for transfers between devices: 58.4 us -> 0.02 us  [shards(): col_panel = lax.all_gather(masked, 'row', axis=0, tiled=True)]
    psum x1 -> x0, blocking collectives: 38.5 us -> none  [shards(): lax.psum((placed, jnp.sum(electron_shape)), ('row', 'col'))]
    pallas_call x1, Pallas kernels: 108 us -> 124 us  [solve(): pl.pallas_call(functools.partial(field_kernel, nrow, ncol, grid, wide), o...]
  transfers between devices with their start and end apart: 2 -> 2, of which waited for: 2 -> 0; matrix products, arithmetic and copies ran while one was open for 0% -> 3% of each run, Pallas kernels for 0% -> 83%
where the time goes in v2:
time: 231 us; the launch traced here: 230 us
  Pallas kernels  192 us (83%)
  between operations  14.8 us (6%)
  matrix products  10.5 us (5%)
  other arithmetic  9.83 us (4%)
    pallas_call x1, Pallas kernels, solve(): pl.pallas_call(functools.partial(field_kernel, nrow, ncol, grid, wide), o...  124 us
    pallas_call x1, Pallas kernels, traces(): pl.pallas_call(functools.partial(trace_kernel, nrow, ncol, blk), out_shap...  68 us
    dot_general x1, matrix products, shards(): square = jnp.dot(row_panel, col_panel, preferred_element_type=F32)  10.5 us
  transfers between devices with their start and end apart: 2, of which 0 were waited for; matrix products, arithmetic and copies ran while one was open for 3% of the time, Pallas kernels for 83%

profile of v2, /device:TPU:9, one launch (start us, length us, event | category | flops | bytes accessed | tf_op | source)
XLA Modules:
  0.0 230.1 jit_solution(13069703373541209363)
XLA Ops:
  7.2 0.0 all-gather.3.cloned.1.call-start
  7.2 0.8 fusion.1
  8.0 0.2 mul.47
  8.2 0.0 copy-start.1
  8.2 2.5 %bitcast_multiply_fusion.1.a_ref = bf16[512,1024]{1,0:T(8,128)(2,1)} fusion(bf16[512,1024]{1,0:T(8,128)(2,1)} %param.9, bf16[64,8,8,128]{3,2,1,0:T(8,128)(2,1)S(1)} %bitcast.19), kind=kLoop, calls=%fused_computation.3 | loop fusion | flops 524288 | bytes 3145728 | tf_op jit(solution)/shard_map/mul | solution.py:410
  10.7 0.0 all-gather.3.cloned.1.call-update
  10.7 0.0 copy-start.3
  10.7 0.0 all-gather.5.cloned.1.call-start
  10.8 0.7 all-gather.5.cloned.1.call-update
  11.5 0.0 copy-done.1
  11.5 1.1 reduce_sum.27
  12.6 0.7 and_select_fusion.part_ref
  13.3 68.0 %shard_map.104 = f32[8,128]{1,0:T(8,128)S(1)} custom-call(bf16[512,1024]{1,0:T(8,128)(2,1)S(1)} %copy-done, f32[8,128]{1,0:T(8,128)S(1)} %and_select_fusion.part_ref), custom_call_target="tpu_custom_call" | custom-call | tf_op jit(solution)/shard_map/pallas_call | solution.py:387
  81.3 0.5 slice.7
  82.5 0.6 slice_reduce_fusion
  83.1 0.6 divide_bitcast_fusion
  83.7 0.2 select_reduce_fusion
  83.9 3.3 %divide_subtract_fusion = f32[32,64,256]{2,1,0:T(8,128)} fusion(f32[32,64,256]{2,1,0:T(8,128)} %param.13, f32[32,64,256]{2,1,0:T(8,128)S(1)} %copy-done.1, f32[]{:T(128)} %bitcast.1, f32[32,64]{1,0:T(8,128)S(1)} %select_reduce_fusion), kind=kLoop, calls=%fused_computation.2 | loop fusion | flops 1572864 | bytes 6299652 | tf_op jit(solution)/shard_map/sub | solution.py:425
  87.2 123.9 %shard_map.105 = f32[2048,256]{1,0:T(8,128)} custom-call(f32[2048,256]{1,0:T(8,128)} %bitcast.17, bf16[2,256,256]{2,1,0:T(8,128)(2,1)} %constant.22.clone.basis_ref, bf16[2,4,128,512]{3,2,1,0:T(8,128)(2,1)} %constant.23.clone.pair_ref, bf16[2,256,256]{2,1,0:T(8,128)(2,1)} %constant.24.clone.first_ref, bf16[2,256,256]{2,1,0:T(8,128)(2,1)} %constant.25.clone.firstt_ref), custom_call_target="tpu_custom_call" | custom-call | tf_op jit(solution)/shard_map/pallas_call | solution.py:262
  211.1 0.0 all-gather.3.cloned.1.call-done
  211.1 0.0 all-gather.5.cloned.1.call-done
  211.1 0.2 mul.52
  211.4 10.5 %fusion = bf16[512,1024]{1,0:T(8,128)(2,1)} fusion(f32[64,8,8,128]{3,2,1,0:T(8,128)S(1)} %bitcast.20, bf16[512,1024]{1,0:T(8,128)(2,1)S(1)} %copy-done, bf16[512,4096]{1,0:T(8,128)(2,1)} %all-gather.3.cloned.1.call-done, bf16[4096,1024]{1,0:T(8,128)(2,1)} %all-gather.5.cloned.1.call-done), kind=kOutput, calls=%fused_computation.1 | convolution fusion | flops 4297588736 | bytes 16777216 | tf_op jit(solution)/shard_map/dot_general | solution.py:427
  221.9 1.3 copy.16
  (7 shorter events, 0.0 us)
Async XLA Ops:
  7.2 203.9 %all-gather.3.cloned.1.call-start = ((), (), s32[]{:S(2)}) async-start(), calls=%async_computation | async-start | bytes 5242880 | tf_op jit(solution)/shard_map/all_gather | solution.py:411
  8.2 3.3 %copy-start.1 = (f32[32,64,256]{2,1,0:T(8,128)S(1)}, f32[32,64,256]{2,1,0:T(8,128)}, u32[]{:S(2)}) copy-start(f32[32,64,256]{2,1,0:T(8,128)} %param.12) | copy-start | bytes 6291460
  10.7 2.7 %copy-start = (bf16[512,1024]{1,0:T(8,128)(2,1)S(1)}, bf16[512,1024]{1,0:T(8,128)(2,1)}, u32[]{:S(2)}) copy-start(bf16[512,1024]{1,0:T(8,128)(2,1)} %bitcast_multiply_fusion.1.a_ref) | copy-start | bytes 3145732
  10.7 73.0 %copy-start.3 = (s32[32,64]{1,0:T(8,128)S(1)}, s32[32,64]{1,0:T(8,128)}, u32[]{:S(2)}) copy-start(s32[32,64]{1,0:T(8,128)} %param.11) | copy-start | bytes 24580
  10.7 200.4 %all-gather.5.cloned.1.call-start = ((), (), s32[]{:S(2)}) async-start(), calls=%async_computation.1 | async-start | bytes 9437184 | tf_op jit(solution)/shard_map/all_gather | solution.py:412
  211.3 10.6 %copy-start.2 = (f32[2048,256]{1,0:T(8,128)S(1)}, f32[2048,256]{1,0:T(8,128)}, u32[]{:S(2)}) copy-start(f32[2048,256]{1,0:T(8,128)} %shard_map.105) | copy-start | bytes 6291460
Sparse Core Ops, SparseCore 0:
  10.8 126.2 all-gather.2
  139.6 68.3 all-gather.4

commit v3 on v2

--- a/solution.py
+++ b/solution.py
@@ -78,8 +78,8 @@
 
 
 def field_kernel(nrow, ncol, grid, wide,
-                 charge_ref, basis_ref, pair_ref, first_ref, firstt_ref, out_ref,
-                 turn, back, *bufs):
+                 charge_ref, basis_ref, pair_ref, first_ref, firstt_ref, block_ref,
+                 out_ref, panel_ref, turn, back, own_sem, far_send, far_recv, near_send, near_recv, *bufs):
     nb = 1 if wide else 2
     stages = [bufs[k * 2 * nb:(k + 1) * 2 * nb] for k in range(4)]
     sems = bufs[8 * nb:]
@@ -99,6 +99,32 @@
         pl.semaphore_signal(barrier, inc=1, device_id={"row": (my_row + t) % nrow}, device_id_type=MESH)
 
     pl.semaphore_wait(barrier, ncol - 1 + nrow - 1)
+
+    chips = nrow // 2
+    my_chip, core = my_row // 2, my_row % 2
+    rows_of = block_ref.shape[0]
+
+    def panel_rows(row):
+        return panel_ref.at[pl.ds(pl.multiple_of(row * rows_of, rows_of), rows_of)]
+
+    def far(chip, slot):
+        return pltpu.make_async_remote_copy(
+            src_ref=block_ref, dst_ref=panel_rows(my_row), send_sem=far_send.at[chip],
+            recv_sem=far_recv.at[slot], device_id={"row": 2 * chip + core}, device_id_type=MESH)
+
+    def near(chip, source):
+        return pltpu.make_async_remote_copy(
+            src_ref=source, dst_ref=panel_rows(2 * chip + core), send_sem=near_send.at[chip],
+            recv_sem=near_recv.at[chip], device_id={"row": 2 * my_chip + 1 - core}, device_id_type=MESH)
+
+    own = pltpu.make_async_copy(block_ref, panel_rows(my_row), own_sem)
+    own.start()
+
+    @pl.loop(1, chips)
+    def _(t):
+        far((my_chip + t) % chips, my_chip).start()
+
+    near(my_chip, block_ref).start()
 
     def copies(stage, axis, me, dest, src):
         res = []
@@ -206,6 +232,12 @@
 
     finish(2, "row", my_row, nrow)
 
+    @pl.loop(1, chips)
+    def _(t):
+        chip = (my_chip + t) % chips
+        far(chip, chip).wait_recv()
+        near(chip, panel_rows(2 * chip + core)).start()
+
     @pl.loop(0, ncol)
     def _(t):
         dest = (my_col + 1 + t) % ncol
@@ -240,14 +272,28 @@
         x = dot_right(back[k], basis_ref[0], basis_ref[1], TN)
         out_ref[pl.ds(pl.multiple_of(k * 128, 128), 128), :] = x * (1.0 / (kappa * kappa))
 
-
-def solve(charge, nrow, ncol, grid, wide):
+    @pl.loop(1, chips)
+    def _(t):
+        far((my_chip + t) % chips, my_chip).wait_send()
+
+    @pl.loop(0, chips)
+    def _(chip):
+        near(chip, block_ref).wait_send()
+        near(chip, block_ref).wait_recv()
+
+    own.wait()
+
+
+def solve(charge, masked, nrow, ncol, grid, wide):
     span_m, span_n = grid // nrow, grid // ncol
     per = 128 // span_n
     groups = span_m // per
     thin = span_n // nrow
     tables = [jnp.asarray(t) for t in make_tables(grid, nrow, ncol)]
     scratch = [pltpu.VMEM((groups, grid, 128), F32), pltpu.VMEM((groups, grid, 128), F32)]
+    scratch.append(pltpu.SemaphoreType.DMA(()))
+    for _ in range(4):
+        scratch.append(pltpu.SemaphoreType.DMA((nrow // 2,)))
     col_shape, row_shape = (ncol, span_n, groups, 128), (nrow, thin, span_m, grid)
     for shape in (col_shape, row_shape, row_shape, col_shape):
         for _ in range(2):
@@ -261,13 +307,14 @@
             scratch.append(pltpu.SemaphoreType.DMA((1 if wide else 2, count)))
     return pl.pallas_call(
         functools.partial(field_kernel, nrow, ncol, grid, wide),
-        out_shape=jax.ShapeDtypeStruct((span_m * span_n, grid), F32),
-        in_specs=[pl.BlockSpec(memory_space=pltpu.VMEM)] * 5,
-        out_specs=pl.BlockSpec(memory_space=pltpu.VMEM),
+        out_shape=(jax.ShapeDtypeStruct((span_m * span_n, grid), F32),
+                   jax.ShapeDtypeStruct((nrow * masked.shape[0], masked.shape[1]), BF16)),
+        in_specs=[pl.BlockSpec(memory_space=pltpu.VMEM)] * 5 + [pl.BlockSpec(memory_space=pl.ANY)],
+        out_specs=(pl.BlockSpec(memory_space=pltpu.VMEM), pl.BlockSpec(memory_space=pl.ANY)),
         scratch_shapes=scratch,
         compiler_params=pltpu.CompilerParams(
             collective_id=0, has_side_effects=True, vmem_limit_bytes=56 * 1024 * 1024),
-    )(charge, *tables)
+    )(charge, *tables, masked)
 
 
 def trace_kernel(nrow, ncol, blk, a_ref, part_ref, out_ref, got, acc, mine, row_in, col_in,
@@ -408,12 +455,12 @@
     nblocks = brows * nrow
     keep = block_mask.astype(BF16)[:, None, :, None]
     masked = (density_matrix.reshape(brows, blk, bcols, blk) * keep).reshape(rows, cols)
-    row_panel = lax.all_gather(masked, "col", axis=1, tiled=True)
-    col_panel = lax.all_gather(masked, "row", axis=0, tiled=True)
     line = jnp.arange(8, dtype=jnp.int32)[:, None]
     lane = jnp.arange(128, dtype=jnp.int32)[None, :]
     part = jnp.where((line == 1) & (lane == 0), jnp.sum(electron_shape), 0.0)
     sums = traces(masked, part, nrow, ncol, blk)
+    later, sums = lax.optimization_barrier((masked, sums))
+    row_panel = lax.all_gather(later, "col", axis=1, tiled=True)
     population, shape_sum = sums[0, :nblocks], sums[1, 0]
     all_ids = jnp.arange(nblocks, dtype=jnp.int32)
     weight = population * nblocks / jnp.sum(population)
@@ -423,7 +470,7 @@
         axis=2,
     )
     charge = cell_weight[:, :, None] * electron_shape / mean_shape - ion_charge
-    potential = solve(charge.reshape(-1, grid), nrow, ncol, grid, WIDE)
+    potential, col_panel = solve(charge.reshape(-1, grid), masked, nrow, ncol, grid, WIDE)
     square = jnp.dot(row_panel, col_panel, preferred_element_type=F32)
     keep_wide = block_mask.astype(F32)[:, None, :, None]
     update = (2.0 * masked.astype(F32) - square).reshape(brows, blk, bcols, blk) * keep_wide

time: 231 us -> 222 us (0.961)
  Pallas kernels: 192 us -> 184 us
    pallas_call x1, Pallas kernels: 68 us -> 44.9 us  [traces(): pl.pallas_call(functools.partial(trace_kernel, nrow, ncol, blk), out_shap...]
    pallas_call x1, Pallas kernels: 124 us -> 139 us  [solve(): pl.pallas_call(functools.partial(field_kernel, nrow, ncol, grid, wide), o...]
  transfers between devices with their start and end apart: 2 -> 1, of which waited for: 0 -> 0; matrix products, arithmetic and copies ran while one was open for 3% -> 2% of each run, Pallas kernels for 83% -> 63%
where the time goes in v3:
time: 222 us; the launch traced here: 221 us
  Pallas kernels  184 us (83%)
  between operations  14.8 us (7%)
  matrix products  10.5 us (5%)
  other arithmetic  8.82 us (4%)
  local copies, waits for them, and re-layouts  3.44 us (2%)
    pallas_call x1, Pallas kernels, solve(): pl.pallas_call(functools.partial(field_kernel, nrow, ncol, grid, wide), o...  139 us
    pallas_call x1, Pallas kernels, traces(): pl.pallas_call(functools.partial(trace_kernel, nrow, ncol, blk), out_shap...  44.9 us
    dot_general x1, matrix products, shards(): square = jnp.dot(row_panel, col_panel, preferred_element_type=F32)  10.5 us
  transfers between devices with their start and end apart: 1, of which 0 were waited for; matrix products, arithmetic and copies ran while one was open for 2% of the time, Pallas kernels for 63%

profile of v3, /device:TPU:9, one launch (start us, length us, event | category | flops | bytes accessed | tf_op | source)
XLA Modules:
  0.0 221.2 jit_solution(7176162129623279324)
XLA Ops:
  7.2 0.0 all-gather.2.cloned.1.call-start
  7.2 0.8 fusion.1
  8.0 0.2 mul.47
  8.2 1.5 bitcast_multiply_fusion.1.a_ref.block_ref
  9.7 0.0 copy-start
  9.7 0.2 copy-done.2
  9.9 1.1 reduce_sum.27
  11.0 0.7 and_select_fusion.part_ref
  11.8 44.9 %shard_map.104 = f32[8,128]{1,0:T(8,128)S(1)} custom-call(bf16[512,1024]{1,0:T(8,128)(2,1)S(1)} %bitcast_multiply_fusion.1.a_ref.block_ref, f32[8,128]{1,0:T(8,128)S(1)} %and_select_fusion.part_ref), custom_call_target="tpu_custom_call" | custom-call | tf_op jit(solution)/shard_map/pallas_call | solution.py:434
  56.7 0.0 copy-done
  56.7 0.0 all-gather.2.cloned.1.call-update
  56.7 0.5 slice.7
  57.9 0.6 slice_reduce_fusion
  58.5 0.6 divide_bitcast_fusion
  59.2 0.0 copy-done.4
  59.2 0.2 select_reduce_fusion
  59.4 3.3 %divide_subtract_fusion = f32[32,64,256]{2,1,0:T(8,128)} fusion(f32[32,64,256]{2,1,0:T(8,128)} %param.13, f32[32,64,256]{2,1,0:T(8,128)S(1)} %copy-done.2, f32[]{:T(128)} %bitcast.1, f32[32,64]{1,0:T(8,128)S(1)} %select_reduce_fusion), kind=kLoop, calls=%fused_computation.2 | loop fusion | flops 1572864 | bytes 6299652 | tf_op jit(solution)/shard_map/sub | solution.py:472
  62.6 138.6 %shard_map.105 = (f32[2048,256]{1,0:T(8,128)}, bf16[4096,1024]{1,0:T(8,128)(2,1)}) custom-call(f32[2048,256]{1,0:T(8,128)} %bitcast.17, bf16[2,256,256]{2,1,0:T(8,128)(2,1)} %constant.22.clone.basis_ref, bf16[2,4,128,512]{3,2,1,0:T(8,128)(2,1)} %constant.23.clone.pair_ref, bf16[2,256,256]{2,1,0:T(8,128)(2,1)} %constant.24.clone.first_ref, ...), custom_call_target="tpu_custom_call" | custom-call | tf_op jit(solution)/shard_map/pallas_call | solution.py:308
  201.2 0.0 copy-start.1
  201.3 0.0 all-gather.2.cloned.1.call-done
  201.3 0.2 mul.56
  201.5 1.0 copy-done.1
  202.5 10.5 %fusion = bf16[512,1024]{1,0:T(8,128)(2,1)} fusion(f32[64,8,8,128]{3,2,1,0:T(8,128)S(1)} %bitcast.19, bf16[512,1024]{1,0:T(8,128)(2,1)S(1)} %copy-done.1, bf16[512,4096]{1,0:T(8,128)(2,1)} %all-gather.2.cloned.1.call-done, bf16[4096,1024]{1,0:T(8,128)(2,1)} %get-tuple-element.8), kind=kOutput, calls=%fused_computation.1 | convolution fusion | flops 4297588736 | bytes 16777216 | tf_op jit(solution)/shard_map/dot_general | solution.py:474
  213.0 1.3 copy.16
  (6 shorter events, 0.0 us)
Async XLA Ops:
  7.2 194.1 %all-gather.2.cloned.1.call-start = ((), (), s32[]{:S(2)}) async-start(), calls=%async_computation | async-start | bytes 5242880 | tf_op jit(solution)/shard_map/all_gather | solution.py:463
  8.0 1.9 copy-start.2
  9.7 47.0 %copy-start = (bf16[512,1024]{1,0:T(8,128)(2,1)}, bf16[512,1024]{1,0:T(8,128)(2,1)S(1)}, u32[]{:S(2)}) copy-start(bf16[512,1024]{1,0:T(8,128)(2,1)S(1)} %bitcast_multiply_fusion.1.a_ref.block_ref) | copy-start | bytes 3145732
  9.9 49.3 %copy-start.4 = (s32[32,64]{1,0:T(8,128)S(1)}, s32[32,64]{1,0:T(8,128)}, u32[]{:S(2)}) copy-start(s32[32,64]{1,0:T(8,128)} %param.11) | copy-start | bytes 24580
  201.2 1.2 copy-start.1
  202.5 10.6 %copy-start.3 = (f32[2048,256]{1,0:T(8,128)S(1)}, f32[2048,256]{1,0:T(8,128)}, u32[]{:S(2)}) copy-start(f32[2048,256]{1,0:T(8,128)} %get-tuple-element.9) | copy-start | bytes 6291460
Sparse Core Ops, SparseCore 0:
  56.9 101.7 all-gather.1

commit v4 on v3

--- a/solution.py
+++ b/solution.py
@@ -68,9 +68,9 @@
 
 def encode(x, value_ref, scale_ref):
     top = jnp.max(jnp.abs(x), axis=1, keepdims=True)
-    unit = jnp.maximum(top, 1e-30) * (1.0 / 32760.0)
-    value_ref[...] = jnp.round(x / unit).astype(jnp.int32).astype(jnp.int16)
-    scale_ref[...] = unit[:, 0, :]
+    top = jnp.maximum(top, 1e-30)
+    value_ref[...] = jnp.round(x * (32760.0 / top)).astype(jnp.int32).astype(jnp.int16)
+    scale_ref[...] = top[:, 0, :] * (1.0 / 32760.0)
 
 
 def decode(value, scale):
@@ -79,7 +79,7 @@
 
 def field_kernel(nrow, ncol, grid, wide,
                  charge_ref, basis_ref, pair_ref, first_ref, firstt_ref, block_ref,
-                 out_ref, panel_ref, turn, back, own_sem, far_send, far_recv, near_send, near_recv, *bufs):
+                 out_ref, panel_ref, turn, back, plain, own_sem, far_send, far_recv, near_send, near_recv, *bufs):
     nb = 1 if wide else 2
     stages = [bufs[k * 2 * nb:(k + 1) * 2 * nb] for k in range(4)]
     sems = bufs[8 * nb:]
@@ -238,13 +238,17 @@
         far(chip, chip).wait_recv()
         near(chip, panel_rows(2 * chip + core)).start()
 
+    @pl.loop(0, nrow)
+    def _(s):
+        plain[s] = get(2, s, slice(None))
+
     @pl.loop(0, ncol)
     def _(t):
         dest = (my_col + 1 + t) % ncol
 
         @pl.loop(0, nrow)
         def _(s):
-            x = get(2, s, slice(None))
+            x = plain[s]
             acc = jnp.zeros((thin * groups, 128), F32)
             for u in range(per):
                 xu = x[:, u * groups:(u + 1) * groups].reshape(thin * groups, grid)
@@ -291,6 +295,7 @@
     thin = span_n // nrow
     tables = [jnp.asarray(t) for t in make_tables(grid, nrow, ncol)]
     scratch = [pltpu.VMEM((groups, grid, 128), F32), pltpu.VMEM((groups, grid, 128), F32)]
+    scratch.append(pltpu.VMEM((nrow, thin, span_m, grid), F32))
     scratch.append(pltpu.SemaphoreType.DMA(()))
     for _ in range(4):
         scratch.append(pltpu.SemaphoreType.DMA((nrow // 2,)))
@@ -317,7 +322,7 @@
     )(charge, *tables, masked)
 
 
-def trace_kernel(nrow, ncol, blk, a_ref, part_ref, out_ref, got, acc, mine, row_in, col_in,
+def trace_kernel(nrow, ncol, blk, a_ref, part_ref, out_ref, got, lines, acc, mine, row_in, col_in,
                  tile_send, tile_recv, row_send, row_recv, col_send, col_recv):
     my_row, my_col = lax.axis_index("row"), lax.axis_index("col")
     rows = a_ref.shape[0]
@@ -365,8 +370,6 @@
             tile_copy(h, other, my_row % ratio).start()
 
     acc[...] = part_ref[...]
-    lane = lax.broadcasted_iota(jnp.int32, acc.shape, 1)
-    line = lax.broadcasted_iota(jnp.int32, acc.shape, 0)
     eye = (lax.broadcasted_iota(jnp.int32, (blk, blk), 0)
            == lax.broadcasted_iota(jnp.int32, (blk, blk), 1))
     for h in range(ratio):
@@ -388,10 +391,15 @@
                         a_ref[g * blk:(g + 1) * blk, h * rows + k * blk:h * rows + (k + 1) * blk],
                         got[h, k * blk:(k + 1) * blk, g * blk:(g + 1) * blk],
                         preferred_element_type=F32)
-                    value = jnp.sum(jnp.where(eye, prod, 0.0))
-                    here = (line == 0) & (lane == my_row * inner + g)
-                    there = (line == 0) & (lane == other * inner + k) & (my_row != other)
-                    acc[...] += jnp.where(here, value, 0.0) + jnp.where(there, value, 0.0)
+                    lines[g * inner + k] = jnp.sum(
+                        jnp.where(eye, prod, 0.0).reshape(blk // 8, 8, blk), axis=0)
+            value = jnp.sum(jnp.sum(lines[...], axis=1, keepdims=True), axis=2, keepdims=True)
+            pair = lax.broadcasted_iota(jnp.int32, (inner * inner, 8, 128), 0)
+            lane3 = lax.broadcasted_iota(jnp.int32, (inner * inner, 8, 128), 2)
+            line3 = lax.broadcasted_iota(jnp.int32, (inner * inner, 8, 128), 1)
+            here = (line3 == 0) & (lane3 == my_row * inner + pair // inner)
+            there = (line3 == 0) & (lane3 == other * inner + pair % inner) & (my_row != other)
+            acc[...] += jnp.sum(jnp.where(here, value, 0.0) + jnp.where(there, value, 0.0), axis=0)
 
     for h in range(ratio):
         other, sends, same = place(h)
@@ -437,7 +445,8 @@
         in_specs=[pl.BlockSpec(memory_space=pltpu.VMEM)] * 2,
         out_specs=pl.BlockSpec(memory_space=pltpu.VMEM),
         scratch_shapes=[
-            pltpu.VMEM((ratio, rows, rows), BF16), pltpu.VMEM(small, F32), pltpu.VMEM(small, F32),
+            pltpu.VMEM((ratio, rows, rows), BF16),
+            pltpu.VMEM(((rows // blk) ** 2, 8, blk), F32), pltpu.VMEM(small, F32), pltpu.VMEM(small, F32),
             pltpu.VMEM((nrow,) + small, F32), pltpu.VMEM((ncol,) + small, F32),
             dma((ratio,)), dma((ratio,)), dma((nrow,)), dma((nrow,)), dma((ncol,)), dma((ncol,)),
         ],

time: 222 us -> 222 us (level)
  no operation moved by 1% of the time
where the time goes in v4:
time: 222 us; the launch traced here: 221 us
  Pallas kernels  184 us (83%)
  between operations  14.8 us (7%)
  matrix products  10.5 us (5%)
  other arithmetic  8.82 us (4%)
  local copies, waits for them, and re-layouts  3.44 us (2%)
    pallas_call x1, Pallas kernels, solve(): pl.pallas_call(functools.partial(field_kernel, nrow, ncol, grid, wide), o...  139 us
    pallas_call x1, Pallas kernels, traces(): pl.pallas_call(functools.partial(trace_kernel, nrow, ncol, blk), out_shap...  44.9 us
    dot_general x1, matrix products, shards(): square = jnp.dot(row_panel, col_panel, preferred_element_type=F32)  10.5 us
  transfers between devices with their start and end apart: 1, of which 0 were waited for; matrix products, arithmetic and copies ran while one was open for 2% of the time, Pallas kernels for 63%

profile of v4, /device:TPU:9, one launch (start us, length us, event | category | flops | bytes accessed | tf_op | source)
XLA Modules:
  0.0 221.3 jit_solution(7421184714191413121)
XLA Ops:
  7.2 0.0 all-gather.2.cloned.1.call-start
  7.2 0.8 fusion.1
  8.0 0.2 mul.47
  8.2 1.5 bitcast_multiply_fusion.1.a_ref.block_ref
  9.7 0.0 copy-start
  9.7 0.2 copy-done.2
  9.9 1.1 reduce_sum.27
  11.0 0.7 and_select_fusion.part_ref
  11.8 44.9 %shard_map.104 = f32[8,128]{1,0:T(8,128)S(1)} custom-call(bf16[512,1024]{1,0:T(8,128)(2,1)S(1)} %bitcast_multiply_fusion.1.a_ref.block_ref, f32[8,128]{1,0:T(8,128)S(1)} %and_select_fusion.part_ref), custom_call_target="tpu_custom_call" | custom-call | tf_op jit(solution)/shard_map/pallas_call | solution.py:442
  56.6 0.0 copy-done
  56.6 0.0 all-gather.2.cloned.1.call-update
  56.7 0.5 slice.7
  57.8 0.6 slice_reduce_fusion
  58.4 0.6 divide_bitcast_fusion
  59.1 0.2 select_reduce_fusion
  59.3 3.3 %divide_subtract_fusion = f32[32,64,256]{2,1,0:T(8,128)} fusion(f32[32,64,256]{2,1,0:T(8,128)} %param.13, f32[32,64,256]{2,1,0:T(8,128)S(1)} %copy-done.2, f32[]{:T(128)} %bitcast.1, f32[32,64]{1,0:T(8,128)S(1)} %select_reduce_fusion), kind=kLoop, calls=%fused_computation.2 | loop fusion | flops 1572864 | bytes 6299652 | tf_op jit(solution)/shard_map/sub | solution.py:481
  62.6 138.8 %shard_map.105 = (f32[2048,256]{1,0:T(8,128)}, bf16[4096,1024]{1,0:T(8,128)(2,1)}) custom-call(f32[2048,256]{1,0:T(8,128)} %bitcast.17, bf16[2,256,256]{2,1,0:T(8,128)(2,1)} %constant.22.clone.basis_ref, bf16[2,4,128,512]{3,2,1,0:T(8,128)(2,1)} %constant.23.clone.pair_ref, bf16[2,256,256]{2,1,0:T(8,128)(2,1)} %constant.24.clone.first_ref, ...), custom_call_target="tpu_custom_call" | custom-call | tf_op jit(solution)/shard_map/pallas_call | solution.py:313
  201.3 0.0 copy-start.1
  201.3 0.0 all-gather.2.cloned.1.call-done
  201.4 0.2 mul.56
  201.6 1.0 copy-done.1
  202.6 10.5 %fusion = bf16[512,1024]{1,0:T(8,128)(2,1)} fusion(f32[64,8,8,128]{3,2,1,0:T(8,128)S(1)} %bitcast.19, bf16[512,1024]{1,0:T(8,128)(2,1)S(1)} %copy-done.1, bf16[512,4096]{1,0:T(8,128)(2,1)} %all-gather.2.cloned.1.call-done, bf16[4096,1024]{1,0:T(8,128)(2,1)} %get-tuple-element.8), kind=kOutput, calls=%fused_computation.1 | convolution fusion | flops 4297588736 | bytes 16777216 | tf_op jit(solution)/shard_map/dot_general | solution.py:483
  213.1 0.0 copy-done.3
  213.1 1.3 copy.16
  (6 shorter events, 0.0 us)
Async XLA Ops:
  7.2 194.2 %all-gather.2.cloned.1.call-start = ((), (), s32[]{:S(2)}) async-start(), calls=%async_computation | async-start | bytes 5242880 | tf_op jit(solution)/shard_map/all_gather | solution.py:472
  8.0 1.9 copy-start.2
  9.7 46.9 %copy-start = (bf16[512,1024]{1,0:T(8,128)(2,1)}, bf16[512,1024]{1,0:T(8,128)(2,1)S(1)}, u32[]{:S(2)}) copy-start(bf16[512,1024]{1,0:T(8,128)(2,1)S(1)} %bitcast_multiply_fusion.1.a_ref.block_ref) | copy-start | bytes 3145732
  9.9 49.2 %copy-start.4 = (s32[32,64]{1,0:T(8,128)S(1)}, s32[32,64]{1,0:T(8,128)}, u32[]{:S(2)}) copy-start(s32[32,64]{1,0:T(8,128)} %param.11) | copy-start | bytes 24580
  201.3 1.2 copy-start.1
  202.6 10.5 %copy-start.3 = (f32[2048,256]{1,0:T(8,128)S(1)}, f32[2048,256]{1,0:T(8,128)}, u32[]{:S(2)}) copy-start(f32[2048,256]{1,0:T(8,128)} %get-tuple-element.9) | copy-start | bytes 6291460
Sparse Core Ops, SparseCore 0:
  56.8 101.7 all-gather.1

commit v5 on v4

--- a/solution.py
+++ b/solution.py
@@ -468,8 +468,7 @@
     lane = jnp.arange(128, dtype=jnp.int32)[None, :]
     part = jnp.where((line == 1) & (lane == 0), jnp.sum(electron_shape), 0.0)
     sums = traces(masked, part, nrow, ncol, blk)
-    later, sums = lax.optimization_barrier((masked, sums))
-    row_panel = lax.all_gather(later, "col", axis=1, tiled=True)
+    row_panel = lax.all_gather(masked, "col", axis=1, tiled=True)
     population, shape_sum = sums[0, :nblocks], sums[1, 0]
     all_ids = jnp.arange(nblocks, dtype=jnp.int32)
     weight = population * nblocks / jnp.sum(population)

time: 222 us -> 226 us (1.018)
  Pallas kernels: 184 us -> 187 us
    pallas_call x1, Pallas kernels: 44.9 us -> 67.9 us  [traces(): pl.pallas_call(functools.partial(trace_kernel, nrow, ncol, blk), out_shap...]
    pallas_call x1, Pallas kernels: 139 us -> 120 us  [solve(): pl.pallas_call(functools.partial(field_kernel, nrow, ncol, grid, wide), o...]
  transfers between devices with their start and end apart: 1 -> 1, of which waited for: 0 -> 0; matrix products, arithmetic and copies ran while one was open for 2% -> 3% of each run, Pallas kernels for 63% -> 83%
where the time goes in v5:
time: 226 us
  Pallas kernels  187 us (83%)
  between operations  14.8 us (7%)
  matrix products  10.5 us (5%)
  other arithmetic  9.83 us (4%)
  local copies, waits for them, and re-layouts  3.24 us (1%)
    pallas_call x1, Pallas kernels, solve(): pl.pallas_call(functools.partial(field_kernel, nrow, ncol, grid, wide), o...  120 us
    pallas_call x1, Pallas kernels, traces(): pl.pallas_call(functools.partial(trace_kernel, nrow, ncol, blk), out_shap...  67.9 us
    dot_general x1, matrix products, shards(): square = jnp.dot(row_panel, col_panel, preferred_element_type=F32)  10.5 us
  transfers between devices with their start and end apart: 1, of which 0 were waited for; matrix products, arithmetic and copies ran while one was open for 3% of the time, Pallas kernels for 83%

profile of v5, /device:TPU:9, one launch (start us, length us, event | category | flops | bytes accessed | tf_op | source)
XLA Modules:
  0.0 225.9 jit_solution(10816460406986279961)
XLA Ops:
  7.2 0.0 all-gather.2.cloned.1.call-start
  7.2 0.8 fusion.1
  8.0 0.2 mul.47
  8.2 0.0 copy-start.2
  8.2 2.5 %bitcast_multiply_fusion.1.a_ref.block_ref = bf16[512,1024]{1,0:T(8,128)(2,1)} fusion(bf16[512,1024]{1,0:T(8,128)(2,1)} %param.9, bf16[64,8,8,128]{3,2,1,0:T(8,128)(2,1)S(1)} %bitcast.18), kind=kLoop, calls=%fused_computation.3 | loop fusion | flops 524288 | bytes 3145728 | tf_op jit(solution)/shard_map/mul | solution.py:466
  10.7 0.0 all-gather.2.cloned.1.call-update
  10.7 0.0 copy-done.2
  10.7 1.1 reduce_sum.27
  11.9 0.7 and_select_fusion.part_ref
  12.6 0.0 copy-done
  12.6 67.9 %shard_map.104 = f32[8,128]{1,0:T(8,128)S(1)} custom-call(bf16[512,1024]{1,0:T(8,128)(2,1)S(1)} %copy-done, f32[8,128]{1,0:T(8,128)S(1)} %and_select_fusion.part_ref), custom_call_target="tpu_custom_call" | custom-call | tf_op jit(solution)/shard_map/pallas_call | solution.py:442
  80.5 0.5 slice.7
  81.7 0.6 slice_reduce_fusion
  82.3 0.6 divide_bitcast_fusion
  82.9 0.0 copy-done.4
  82.9 0.2 select_reduce_fusion
  83.1 3.3 %divide_subtract_fusion = f32[32,64,256]{2,1,0:T(8,128)} fusion(f32[32,64,256]{2,1,0:T(8,128)} %param.13, f32[32,64,256]{2,1,0:T(8,128)S(1)} %copy-done.2, f32[]{:T(128)} %bitcast.1, f32[32,64]{1,0:T(8,128)S(1)} %select_reduce_fusion), kind=kLoop, calls=%fused_computation.2 | loop fusion | flops 1572864 | bytes 6299652 | tf_op jit(solution)/shard_map/sub | solution.py:480
  86.4 119.5 %shard_map.105 = (f32[2048,256]{1,0:T(8,128)}, bf16[4096,1024]{1,0:T(8,128)(2,1)}) custom-call(f32[2048,256]{1,0:T(8,128)} %bitcast.17, bf16[2,256,256]{2,1,0:T(8,128)(2,1)} %constant.22.clone.basis_ref, bf16[2,4,128,512]{3,2,1,0:T(8,128)(2,1)} %constant.23.clone.pair_ref, bf16[2,256,256]{2,1,0:T(8,128)(2,1)} %constant.24.clone.first_ref, ...), custom_call_target="tpu_custom_call" | custom-call | tf_op jit(solution)/shard_map/pallas_call | solution.py:313
  205.9 0.0 copy-start.1
  205.9 0.0 all-gather.2.cloned.1.call-done
  206.0 0.2 mul.56
  206.2 1.0 copy-done.1
  207.2 10.5 %fusion = bf16[512,1024]{1,0:T(8,128)(2,1)} fusion(f32[64,8,8,128]{3,2,1,0:T(8,128)S(1)} %bitcast.19, bf16[512,1024]{1,0:T(8,128)(2,1)S(1)} %copy-done.1, bf16[512,4096]{1,0:T(8,128)(2,1)} %all-gather.2.cloned.1.call-done, bf16[4096,1024]{1,0:T(8,128)(2,1)} %get-tuple-element.4), kind=kOutput, calls=%fused_computation.1 | convolution fusion | flops 4297588736 | bytes 16777216 | tf_op jit(solution)/shard_map/dot_general | solution.py:482
  217.7 1.3 copy.16
  (6 shorter events, 0.0 us)
Async XLA Ops:
  7.2 198.8 %all-gather.2.cloned.1.call-start = ((), (), s32[]{:S(2)}) async-start(), calls=%async_computation | async-start | bytes 5242880 | tf_op jit(solution)/shard_map/all_gather | solution.py:471
  8.2 2.5 %copy-start.2 = (f32[32,64,256]{2,1,0:T(8,128)S(1)}, f32[32,64,256]{2,1,0:T(8,128)}, u32[]{:S(2)}) copy-start(f32[32,64,256]{2,1,0:T(8,128)} %param.12) | copy-start | bytes 6291460
  10.7 1.9 copy-start
  10.7 72.2 %copy-start.4 = (s32[32,64]{1,0:T(8,128)S(1)}, s32[32,64]{1,0:T(8,128)}, u32[]{:S(2)}) copy-start(s32[32,64]{1,0:T(8,128)} %param.11) | copy-start | bytes 24580
  205.9 1.2 copy-start.1
  207.2 10.5 %copy-start.3 = (f32[2048,256]{1,0:T(8,128)S(1)}, f32[2048,256]{1,0:T(8,128)}, u32[]{:S(2)}) copy-start(f32[2048,256]{1,0:T(8,128)} %get-tuple-element.5) | copy-start | bytes 6291460
Sparse Core Ops, SparseCore 0:
  10.8 125.4 all-gather.1
